TPU v7x, 512 devices: a whole 4x4x16 slice. The times are simulated.
512 devices in a mesh: src: 32 (over z, core), tgt: 16 (over x, y).
Axes of the slice: x: 4, y: 4, z: 16, core: 2. Of those that a mesh axis runs over, the one named last changes fastest.
Arguments:
- source_latents: bfloat16 [16384, 1024], P('src'), may hold values from -32 to 32
- target_latents: bfloat16 [16384, 1024], P('tgt'), may hold values from -32 to 32
Outputs:
- transported_targets: bfloat16 [16384, 1024], P('src', 'tgt')
- source_potential: float32 [16384], P('src')
- target_potential: float32 [16384], P('tgt')
All inputs are finite; a program needn't handle non-finite values.
Results may differ from a plain program's by a relative error of at most 0.018.
Values may be sent and summed in bfloat16 or wider, within the bound.
A program may use at most 64 MiB of HBM per device.

v0:
```python
import math

import jax
import jax.numpy as jnp
from jax import lax
from jax.sharding import PartitionSpec as P

ITERS = 3


def collapse_target_axis(kernel_exponent_array):
    local_peak = jnp.max(kernel_exponent_array, axis=1)
    top_score = lax.pmax(local_peak, "tgt")
    exp_total = lax.psum(
        jnp.sum(jnp.exp(kernel_exponent_array - top_score[:, None]), axis=1), "tgt"
    )
    return top_score + jnp.log(exp_total)


def collapse_source_axis(kernel_exponent_array):
    local_peak = jnp.max(kernel_exponent_array, axis=0)
    top_score = lax.pmax(local_peak, "src")
    exp_total = lax.psum(
        jnp.sum(jnp.exp(kernel_exponent_array - top_score[None, :]), axis=0), "src"
    )
    return top_score + jnp.log(exp_total)


def local(source_latents, target_latents):
    row_count_total = source_latents.shape[0] * lax.axis_size("src")
    column_count_total = target_latents.shape[0] * lax.axis_size("tgt")
    embedding_dimension = source_latents.shape[1]
    regularizer_strength = 1.28 / math.sqrt(embedding_dimension)
    source_sq = (
        jnp.sum(jnp.square(source_latents.astype(jnp.float32)), axis=1) / embedding_dimension
    )
    target_sq = (
        jnp.sum(jnp.square(target_latents.astype(jnp.float32)), axis=1) / embedding_dimension
    )
    cross_term = jnp.einsum(
        "sk,tk->st", source_latents, target_latents, preferred_element_type=jnp.float32
    )
    pairwise_price_piece = (
        source_sq[:, None] + target_sq[None, :] - 2.0 / embedding_dimension * cross_term
    )
    target_dual_variable = jnp.zeros((target_latents.shape[0],), jnp.float32)
    source_dual_variable = jnp.zeros((source_latents.shape[0],), jnp.float32)
    for sweep_index in range(ITERS):
        source_dual_variable = -regularizer_strength * math.log(
            column_count_total
        ) - regularizer_strength * collapse_target_axis(
            (target_dual_variable[None, :] - pairwise_price_piece) / regularizer_strength
        )
        target_dual_variable = -regularizer_strength * math.log(
            row_count_total
        ) - regularizer_strength * collapse_source_axis(
            (source_dual_variable[:, None] - pairwise_price_piece) / regularizer_strength
        )
    kernel_exponent_array = (
        target_dual_variable[None, :] - pairwise_price_piece
    ) / regularizer_strength
    row_level = collapse_target_axis(kernel_exponent_array)
    weights = jnp.exp(kernel_exponent_array - row_level[:, None]).astype(jnp.bfloat16)
    partial_sums = jnp.dot(weights, target_latents, preferred_element_type=jnp.float32)
    transported = lax.psum_scatter(
        partial_sums.astype(jnp.bfloat16), "tgt", scatter_dimension=1, tiled=True
    )
    return (transported, source_dual_variable, target_dual_variable)


def solution(mesh):
    placed = (P("src", None), P("tgt", None))
    return jax.shard_map(
        local,
        mesh=mesh,
        in_specs=placed,
        out_specs=(P("src", "tgt"), P("src"), P("tgt")),
        check_vma=False,
    )
```

profile of v0, /device:TPU:1, one launch (start us, length us, event | category | flops | bytes accessed | tf_op | source)
XLA Modules:
  0.0 687.2 jit_solution(6492248229890227284)
XLA Ops:
  7.2 0.0 copy-start.1
  7.2 0.0 reduce-scatter.2.cloned.1.call-start
  7.2 0.0 copy-start
  7.2 1.7 multiply_reduce_fusion.1
  8.9 2.1 multiply_reduce_fusion
  11.0 0.0 copy-done.1
  11.0 0.0 copy-done
  11.0 1.6 fusion
  12.6 34.3 %pmax.49 = f32[512]{0:T(512)S(1)} all-reduce(f32[512]{0:T(512)S(1)} %get-tuple-element.3), channel_id=1, replica_groups=mesh['src'=32,'tgt'=16] {'tgt'}, use_global_device_ids=true, to_apply=%region_3.0 | all-reduce | flops 512 | bytes 4096 | tf_op jit(solution)/shard_map/pmax | solution.py:13
  46.8 0.6 exponential_reduce_fusion.6
  47.4 28.5 %psum.49 = f32[512]{0:T(512)S(1)} all-reduce(f32[512]{0:T(512)S(1)} %exponential_reduce_fusion.6), channel_id=1, replica_groups=mesh['src'=32,'tgt'=16] {'tgt'}, use_global_device_ids=true, to_apply=%region_5.0 | all-reduce | flops 512 | bytes 4096 | tf_op jit(solution)/shard_map/psum | solution.py:14
  75.9 0.3 fusion.1
  76.2 66.7 %pmax.50 = f32[1024]{0:T(1024)S(1)} all-reduce(f32[1024]{0:T(1024)S(1)} %fusion.1), channel_id=1, replica_groups=mesh['src'=32,'tgt'=16] {'src'}, use_global_device_ids=true, to_apply=%region_7.0 | all-reduce | flops 1024 | bytes 8192 | tf_op jit(solution)/shard_map/pmax | solution.py:22
  142.9 0.5 exponential_reduce_fusion.5
  143.4 45.3 %psum.50 = f32[1024]{0:T(1024)S(1)} all-reduce(f32[1024]{0:T(1024)S(1)} %exponential_reduce_fusion.5), channel_id=1, replica_groups=mesh['src'=32,'tgt'=16] {'src'}, use_global_device_ids=true, to_apply=%region_9.0 | all-reduce | flops 1024 | bytes 8192 | tf_op jit(solution)/shard_map/psum | solution.py:23
  188.7 0.3 fusion.2
  189.0 30.2 %pmax.51 = f32[512]{0:T(512)S(1)} all-reduce(f32[512]{0:T(512)S(1)} %fusion.2), channel_id=1, replica_groups=mesh['src'=32,'tgt'=16] {'tgt'}, use_global_device_ids=true, to_apply=%region_11.0 | all-reduce | flops 512 | bytes 4096 | tf_op jit(solution)/shard_map/pmax | solution.py:13
  219.2 0.6 exponential_reduce_fusion.4
  219.8 28.5 %psum.51 = f32[512]{0:T(512)S(1)} all-reduce(f32[512]{0:T(512)S(1)} %exponential_reduce_fusion.4), channel_id=1, replica_groups=mesh['src'=32,'tgt'=16] {'tgt'}, use_global_device_ids=true, to_apply=%region_13.0 | all-reduce | flops 512 | bytes 4096 | tf_op jit(solution)/shard_map/psum | solution.py:14
  248.3 0.3 fusion.3
  248.6 60.3 %pmax.52 = f32[1024]{0:T(1024)S(1)} all-reduce(f32[1024]{0:T(1024)S(1)} %fusion.3), channel_id=1, replica_groups=mesh['src'=32,'tgt'=16] {'src'}, use_global_device_ids=true, to_apply=%region_15.0 | all-reduce | flops 1024 | bytes 8192 | tf_op jit(solution)/shard_map/pmax | solution.py:22
  308.9 0.5 exponential_reduce_fusion.3
  309.4 45.8 %psum.52 = f32[1024]{0:T(1024)S(1)} all-reduce(f32[1024]{0:T(1024)S(1)} %exponential_reduce_fusion.3), channel_id=1, replica_groups=mesh['src'=32,'tgt'=16] {'src'}, use_global_device_ids=true, to_apply=%region_17.0 | all-reduce | flops 1024 | bytes 8192 | tf_op jit(solution)/shard_map/psum | solution.py:23
  355.3 0.3 fusion.4
  355.5 30.2 %pmax.53 = f32[512]{0:T(512)S(1)} all-reduce(f32[512]{0:T(512)S(1)} %fusion.4), channel_id=1, replica_groups=mesh['src'=32,'tgt'=16] {'tgt'}, use_global_device_ids=true, to_apply=%region_19.0 | all-reduce | flops 512 | bytes 4096 | tf_op jit(solution)/shard_map/pmax | solution.py:13
  385.8 0.6 exponential_reduce_fusion.2
  386.3 28.5 %psum.53 = f32[512]{0:T(512)S(1)} all-reduce(f32[512]{0:T(512)S(1)} %exponential_reduce_fusion.2), channel_id=1, replica_groups=mesh['src'=32,'tgt'=16] {'tgt'}, use_global_device_ids=true, to_apply=%region_21.0 | all-reduce | flops 512 | bytes 4096 | tf_op jit(solution)/shard_map/psum | solution.py:14
  414.8 0.0 copy-start.3
  414.9 0.3 fusion.5
  415.1 60.0 %pmax.54 = f32[1024]{0:T(1024)S(1)} all-reduce(f32[1024]{0:T(1024)S(1)} %fusion.5), channel_id=1, replica_groups=mesh['src'=32,'tgt'=16] {'src'}, use_global_device_ids=true, to_apply=%region_23.0 | all-reduce | flops 1024 | bytes 8192 | tf_op jit(solution)/shard_map/pmax | solution.py:22
  475.1 0.5 exponential_reduce_fusion.1
  475.6 0.0 copy-done.3
  475.6 45.8 %psum.54 = f32[1024]{0:T(1024)S(1)} all-reduce(f32[1024]{0:T(1024)S(1)} %exponential_reduce_fusion.1), channel_id=1, replica_groups=mesh['src'=32,'tgt'=16] {'src'}, use_global_device_ids=true, to_apply=%region_25.0 | all-reduce | flops 1024 | bytes 8192 | tf_op jit(solution)/shard_map/psum | solution.py:23
  521.5 0.0 copy-start.2
  521.5 0.3 fusion.6
  521.7 30.2 %pmax.55 = f32[512]{0:T(512)S(1)} all-reduce(f32[512]{0:T(512)S(1)} %fusion.6), channel_id=1, replica_groups=mesh['src'=32,'tgt'=16] {'tgt'}, use_global_device_ids=true, to_apply=%region_27.0 | all-reduce | flops 512 | bytes 4096 | tf_op jit(solution)/shard_map/pmax | solution.py:13
  552.0 0.6 exponential_reduce_fusion
  552.5 28.5 %psum.55 = f32[512]{0:T(512)S(1)} all-reduce(f32[512]{0:T(512)S(1)} %exponential_reduce_fusion), channel_id=1, replica_groups=mesh['src'=32,'tgt'=16] {'tgt'}, use_global_device_ids=true, to_apply=%region_29.0 | all-reduce | flops 512 | bytes 4096 | tf_op jit(solution)/shard_map/psum | solution.py:14
  581.1 0.0 copy-done.2
  581.1 4.0 convolution_convert_fusion
  585.0 0.0 reduce-scatter.2.cloned.1.call-update
  585.1 95.3 %reduce-scatter.2.cloned.1.call-done = bf16[512,64]{0,1:T(8,128)(2,1)} async-done(((bf16[512,1024]{0,1:T(8,128)(2,1)}), bf16[512,64]{0,1:T(8,128)(2,1)}) %reduce-scatter.2.cloned.1.call-update) | async-done | bytes 65552 | tf_op jit(solution)/shard_map/reduce_scatter | solution.py:65
  (9 shorter events, 0.1 us)
Async XLA Ops:
  7.2 3.8 copy-start.1
  7.2 673.2 %reduce-scatter.2.cloned.1.call-start = ((), (), s32[]{:S(2)}) async-start(), calls=%async_computation.1 | async-start | bytes 1114112 | tf_op jit(solution)/shard_map/reduce_scatter | solution.py:65
  7.2 3.8 copy-start
  414.8 60.8 %copy-start.3 = (f32[512]{0:T(512)}, f32[512]{0:T(512)S(1)}, u32[]{:S(2)}) copy-start(f32[512]{0:T(512)S(1)} %multiply_subtract_fusion.4) | copy-start | bytes 6148
  521.5 59.6 %copy-start.2 = (f32[1024]{0:T(1024)}, f32[1024]{0:T(1024)S(1)}, u32[]{:S(2)}) copy-start(f32[1024]{0:T(1024)S(1)} %multiply_subtract_fusion.1) | copy-start | bytes 12292
Sparse Core Ops, SparseCore 0:
  585.2 95.1 reduce-scatter.1
where the time goes:
time: 688 us; the launch traced here: 687 us
  blocking collectives  563 us (82%)
  waiting for transfers between devices  95.4 us (14%)
  between operations  14.1 us (2%)
  other arithmetic  9.24 us (1%)
    pmax x3, blocking collectives, collapse_source_axis(): top_score = lax.pmax(local_peak, 'src')  187 us
    psum x3, blocking collectives, collapse_source_axis(): lax.psum(jnp.sum(jnp.exp(kernel_exponent_array - top_score[None, :]), axi...  137 us
    pmax x4, blocking collectives, collapse_target_axis(): top_score = lax.pmax(local_peak, 'tgt')  125 us
    psum x4, blocking collectives, collapse_target_axis(): lax.psum(jnp.sum(jnp.exp(kernel_exponent_array - top_score[:, None]), axi...  114 us
    reduce_scatter x1, waiting for transfers between devices, local(): lax.psum_scatter(partial_sums.astype(jnp.bfloat16), 'tgt', scatter_dimens...  95.3 us
  transfers between devices with their start and end apart: 1, of which 1 were waited for; matrix products, arithmetic and copies ran while one was open for 0% of the time, Pallas kernels for 0%

commit v1 on v0

v1 whole, which is shorter than its diff:
```python
import functools
import math

import jax
import jax.numpy as jnp
from jax import lax
from jax.experimental import pallas as pl
from jax.experimental.pallas import tpu as pltpu
from jax.sharding import PartitionSpec as P

ITERS = 3
LOG2E = math.log2(math.e)
LANES = 128
F32 = jnp.float32
BF16 = jnp.bfloat16
NT_DIMS = (((1,), (1,)), ((), ()))


def ring_distance(k, n):
    return min(k, n - k)


def log2(x):
    return jnp.log(x) * LOG2E


def combine(parts):
    top = functools.reduce(jnp.maximum, parts)
    total = functools.reduce(jnp.add, [jnp.exp2(p - top) for p in parts])
    return top + log2(total)


def square_sums(block_ref, start, out_ref, row):
    width = block_ref.shape[1]
    total = jnp.zeros((LANES, LANES), F32)
    for c in range(width // LANES):
        piece = block_ref[pl.ds(start, LANES), c * LANES : (c + 1) * LANES].astype(F32)
        total = total + piece * piece
    out_ref[row : row + 1, :] = jnp.sum(total.T, axis=0, keepdims=True)


def kernel(
    cfg,
    src_hbm,
    tgt_hbm,
    moved_ref,
    f_ref,
    g_ref,
    a,
    b,
    b_t,
    scores,
    part,
    column,
    weights,
    sums,
    arrived,
    h_ref,
    u_ref,
    ss_ref,
    tt_ref,
    peak_ref,
    mass_ref,
    own_lse,
    t_send,
    t_recv,
    c_send,
    c_recv,
    z_send,
    z_recv,
    load_sem,
    t_ssem,
    t_rsem,
    c_ssem,
    c_rsem,
    z_ssem,
    z_rsem,
    m_ssem,
    m_rsem,
):
    n_z, n_x, n_y, eps, log2_rows, log2_cols = cfg
    rows, depth = a.shape
    cols = b.shape[0]
    row_groups, col_groups = rows // LANES, cols // LANES
    s_me, t_me = lax.axis_index("src"), lax.axis_index("tgt")
    z_me, core_me = s_me // 2, s_me % 2
    x_me, y_me = t_me // n_y, t_me % n_y
    feats = depth // (n_x * n_y)

    z_peers = []
    for k in sorted(range(1, n_z), key=lambda k: -ring_distance(k, n_z)):
        z_peers.append({"src": ((z_me + k) % n_z) * 2 + core_me, "tgt": t_me})
    sibling = {"src": z_me * 2 + (1 - core_me), "tgt": t_me}
    steps = [(dx, dy) for dx in range(n_x) for dy in range(n_y) if dx or dy]
    steps.sort(key=lambda d: (-ring_distance(d[0], n_x), -ring_distance(d[1], n_y)))
    t_index = [((x_me + dx) % n_x) * n_y + (y_me + dy) % n_y for dx, dy in steps]
    far = sorted(
        range(len(steps)),
        key=lambda k: -ring_distance(steps[k][0], n_x) - ring_distance(steps[k][1], n_y),
    )

    barrier = pltpu.get_barrier_semaphore()
    everyone = z_peers + [{"src": s_me, "tgt": t_index[k]} for k in far] + [sibling]
    for peer in everyone:
        pl.semaphore_signal(
            barrier, inc=1, device_id=peer, device_id_type=pl.DeviceIdType.MESH
        )

    quarter = cols // 4
    loads = [pltpu.make_async_copy(src_hbm, a, load_sem.at[4])]
    for q in range(4):
        piece = pl.ds(q * quarter, quarter)
        loads.append(pltpu.make_async_copy(tgt_hbm.at[piece], b.at[piece], load_sem.at[q]))
    for copy in loads:
        copy.start()
    loads[0].wait()
    for q in range(4):
        loads[1 + q].wait()
        dot = lax.dot_general(
            a[...],
            b[q * quarter : (q + 1) * quarter, :],
            NT_DIMS,
            preferred_element_type=F32,
        )
        scores[:, q * quarter : (q + 1) * quarter] = dot * (2.0 * LOG2E / (depth * eps))
        for k in range(quarter // LANES):
            block = q * (quarter // LANES) + k
            square_sums(b, block * LANES, tt_ref, block)
    h_ref[...] = tt_ref[...] * (-LOG2E / (depth * eps))

    def rows_pass(out_ref):
        shift = [
            jnp.broadcast_to(h_ref[c : c + 1, :], (8, LANES)) for c in range(col_groups)
        ]

        def some_rows(block, carry):
            for k in range(4):
                at = pl.ds(pl.multiple_of(block * 32 + k * 8, 8), 8)
                v = [
                    scores[at, c * LANES : (c + 1) * LANES] + shift[c]
                    for c in range(col_groups)
                ]
                part[at, :] = combine(v)
            return carry

        lax.fori_loop(0, rows // 32, some_rows, 0)
        for r in range(row_groups):
            x = part[r * LANES : (r + 1) * LANES, :].T
            top = jnp.max(x, axis=0, keepdims=True)
            out_ref[r : r + 1, :] = top + log2(
                jnp.sum(jnp.exp2(x - top), axis=0, keepdims=True)
            )

    def to_column(ref):
        for r in range(row_groups):
            column[r * LANES : (r + 1) * LANES, :] = jnp.broadcast_to(
                ref[r : r + 1, :], (LANES, LANES)
            ).T

    def start_rows_exchange(i):
        for k in far:
            pltpu.make_async_remote_copy(
                src_ref=t_send.at[i],
                dst_ref=t_recv.at[i, k],
                send_sem=t_ssem.at[i],
                recv_sem=t_rsem.at[i],
                device_id={"src": s_me, "tgt": t_index[k]},
                device_id_type=pl.DeviceIdType.MESH,
            ).start()

    def wait_bytes(ref, sem):
        pltpu.make_async_copy(ref, ref, sem).wait()

    def columns_pass(out_ref):
        shape = (8, LANES)
        low = jnp.full(shape, -3.0e38, F32)
        start = tuple([low] * col_groups + [jnp.zeros(shape, F32)] * col_groups)

        def some_rows(block, carry):
            tops, totals = list(carry[:col_groups]), list(carry[col_groups:])
            at = [pl.ds(pl.multiple_of(block * 64 + k * 8, 8), 8) for k in range(8)]
            u = [column[p, :] for p in at]
            for c in range(col_groups):
                v = [scores[p, c * LANES : (c + 1) * LANES] + w for p, w in zip(at, u)]
                top = functools.reduce(jnp.maximum, v + [tops[c]])
                mass = functools.reduce(jnp.add, [jnp.exp2(p - top) for p in v])
                totals[c] = totals[c] * jnp.exp2(tops[c] - top) + mass
                tops[c] = top
            return tuple(tops + totals)

        done = lax.fori_loop(0, rows // 64, some_rows, start)
        for c in range(col_groups):
            peak_ref[c * 8 : (c + 1) * 8, :] = done[c]
            mass_ref[c * 8 : (c + 1) * 8, :] = done[col_groups + c]
        peaks = [peak_ref[pl.ds(r, col_groups, stride=8), :] for r in range(8)]
        masses = [mass_ref[pl.ds(r, col_groups, stride=8), :] for r in range(8)]
        top = functools.reduce(jnp.maximum, peaks)
        total = functools.reduce(
            jnp.add, [m * jnp.exp2(p - top) for p, m in zip(peaks, masses)]
        )
        out_ref[...] = top + log2(total)

    def sweep(i, carry):
        rows_pass(t_send.at[i])

        @pl.when(i == 0)
        def _():
            pl.semaphore_wait(barrier, len(everyone))

        start_rows_exchange(i)

        @pl.when(i == 0)
        def _():
            for r in range(row_groups):
                square_sums(a, r * LANES, ss_ref, r)

            def turn(block, carry):
                at = pl.ds(pl.multiple_of(block * LANES, LANES), LANES)
                for c in range(depth // LANES):
                    b_t[c * LANES : (c + 1) * LANES, at] = b[
                        at, c * LANES : (c + 1) * LANES
                    ].T
                return carry

            lax.fori_loop(0, col_groups, turn, 0)

        wait_bytes(t_recv.at[i], t_rsem.at[i])
        u_ref[...] = -log2_cols - combine(
            [t_send[i]] + [t_recv[i, k] for k in range(len(steps))]
        )
        to_column(u_ref)
        columns_pass(c_send.at[i])
        copy = pltpu.make_async_remote_copy(
            src_ref=c_send.at[i],
            dst_ref=c_recv.at[i],
            send_sem=c_ssem.at[i],
            recv_sem=c_rsem.at[i],
            device_id=sibling,
            device_id_type=pl.DeviceIdType.MESH,
        )
        copy.start()
        copy.wait_recv()
        z_send[i] = combine([c_send[i], c_recv[i]])
        for k, peer in enumerate(z_peers):
            pltpu.make_async_remote_copy(
                src_ref=z_send.at[i],
                dst_ref=z_recv.at[i, k],
                send_sem=z_ssem.at[i],
                recv_sem=z_rsem.at[i],
                device_id=peer,
                device_id_type=pl.DeviceIdType.MESH,
            ).start()
        wait_bytes(z_recv.at[i], z_rsem.at[i])
        h_ref[...] = -log2_rows - combine(
            [z_send[i]] + [z_recv[i, k] for k in range(len(z_peers))]
        )
        return carry

    lax.fori_loop(0, ITERS, sweep, 0)

    rows_pass(t_send.at[ITERS])
    start_rows_exchange(ITERS)
    to_column(t_send.at[ITERS])
    shift = [
        jnp.broadcast_to(h_ref[c : c + 1, :], (16, LANES)) for c in range(col_groups)
    ]

    def some_weights(block, carry):
        for k in range(2):
            at = pl.ds(pl.multiple_of(block * 32 + k * 16, 16), 16)
            level = column[at, :]
            for c in range(col_groups):
                v = scores[at, c * LANES : (c + 1) * LANES] + shift[c]
                weights[at, c * LANES : (c + 1) * LANES] = jnp.exp2(v - level).astype(BF16)
        return carry

    lax.fori_loop(0, rows // 32, some_weights, 0)

    per_x = n_y * feats
    for dx in sorted(range(n_x), key=lambda d: -ring_distance(d, n_x)):
        start = pl.multiple_of(((x_me + dx) % n_x) * per_x, per_x)
        dot = lax.dot_general(
            b_t[pl.ds(start, per_x), :],
            weights[...],
            NT_DIMS,
            preferred_element_type=F32,
        )
        sums[pl.ds(start, per_x), :] = dot.astype(BF16)
        for k, step in enumerate(steps):
            if step[0] == dx:
                pltpu.make_async_remote_copy(
                    src_ref=sums.at[
                        pl.ds(pl.multiple_of(t_index[k] * feats, feats), feats)
                    ],
                    dst_ref=arrived.at[k],
                    send_sem=m_ssem.at[k],
                    recv_sem=m_rsem.at[k],
                    device_id={"src": s_me, "tgt": t_index[k]},
                    device_id_type=pl.DeviceIdType.MESH,
                ).start()

    f_ref[...] = ss_ref[...] * (1.0 / depth) + u_ref[...] * (eps / LOG2E)
    g_ref[...] = tt_ref[...] * (1.0 / depth) + h_ref[...] * (eps / LOG2E)

    wait_bytes(t_recv.at[ITERS], t_rsem.at[ITERS])
    level = combine([t_send[ITERS]] + [t_recv[ITERS, k] for k in range(len(steps))])
    own_lse[...] = jnp.exp2(t_send[ITERS] - level)
    for k in range(len(steps)):
        t_recv[ITERS, k] = jnp.exp2(t_recv[ITERS, k] - level)
    mine = pl.ds(pl.multiple_of(t_me * feats, feats), feats)
    for r in range(row_groups):
        lane = slice(r * LANES, (r + 1) * LANES)
        moved_ref[:, lane] = sums[mine, lane].astype(F32) * own_lse[r : r + 1, :]
    for k in sorted(
        range(len(steps)),
        key=lambda k: ring_distance(steps[k][0], n_x) + ring_distance(steps[k][1], n_y),
    ):
        wait_bytes(arrived.at[k], m_rsem.at[k])
        for r in range(row_groups):
            lane = slice(r * LANES, (r + 1) * LANES)
            moved_ref[:, lane] += (
                arrived[k, :, lane].astype(F32) * t_recv[ITERS, k, r : r + 1, :]
            )

    for i in range(ITERS):
        wait_bytes(c_send.at[i], c_ssem.at[i])
        wait_bytes(z_recv.at[i], z_ssem.at[i])
    for i in range(ITERS + 1):
        wait_bytes(t_recv.at[i], t_ssem.at[i])
    for k in range(len(steps)):
        wait_bytes(arrived.at[k], m_ssem.at[k])


def local(cfg, source_latents, target_latents):
    n_z, n_x, n_y = cfg[:3]
    rows, depth = source_latents.shape
    cols = target_latents.shape[0]
    feats = depth // (n_x * n_y)
    row_groups, col_groups = rows // LANES, cols // LANES
    t_peers, z_peers = n_x * n_y - 1, n_z - 1
    vmem = pl.BlockSpec(memory_space=pltpu.VMEM)
    hbm = pl.BlockSpec(memory_space=pl.ANY)
    dma = pltpu.SemaphoreType.DMA
    moved, f, g = pl.pallas_call(
        functools.partial(kernel, cfg),
        out_shape=(
            jax.ShapeDtypeStruct((feats, rows), F32),
            jax.ShapeDtypeStruct((row_groups, LANES), F32),
            jax.ShapeDtypeStruct((col_groups, LANES), F32),
        ),
        in_specs=[hbm, hbm],
        out_specs=(vmem, vmem, vmem),
        scratch_shapes=[
            pltpu.VMEM((rows, depth), BF16),
            pltpu.VMEM((cols, depth), BF16),
            pltpu.VMEM((depth, cols), BF16),
            pltpu.VMEM((rows, cols), F32),
            pltpu.VMEM((rows, LANES), F32),
            pltpu.VMEM((rows, LANES), F32),
            pltpu.VMEM((rows, cols), BF16),
            pltpu.VMEM((depth, rows), BF16),
            pltpu.VMEM((t_peers, feats, rows), BF16),
            pltpu.VMEM((col_groups, LANES), F32),
            pltpu.VMEM((row_groups, LANES), F32),
            pltpu.VMEM((row_groups, LANES), F32),
            pltpu.VMEM((col_groups, LANES), F32),
            pltpu.VMEM((col_groups * 8, LANES), F32),
            pltpu.VMEM((col_groups * 8, LANES), F32),
            pltpu.VMEM((row_groups, LANES), F32),
            pltpu.VMEM((ITERS + 1, row_groups, LANES), F32),
            pltpu.VMEM((ITERS + 1, t_peers, row_groups, LANES), F32),
            pltpu.VMEM((ITERS, col_groups, LANES), F32),
            pltpu.VMEM((ITERS, col_groups, LANES), F32),
            pltpu.VMEM((ITERS, col_groups, LANES), F32),
            pltpu.VMEM((ITERS, z_peers, col_groups, LANES), F32),
            dma((5,)),
            dma((ITERS + 1,)),
            dma((ITERS + 1,)),
            dma((ITERS,)),
            dma((ITERS,)),
            dma((ITERS,)),
            dma((ITERS,)),
            dma((t_peers,)),
            dma((t_peers,)),
        ],
        compiler_params=pltpu.CompilerParams(
            collective_id=0, has_side_effects=True, vmem_limit_bytes=40 << 20
        ),
        name="transport",
    )(source_latents, target_latents)
    return moved.T.astype(BF16), f.reshape(rows), g.reshape(cols)


def solution(mesh):
    n_src, n_tgt = mesh.shape["src"], mesh.shape["tgt"]
    n_x = math.isqrt(n_tgt)

    def whole(source_latents, target_latents):
        eps = 1.28 / math.sqrt(source_latents.shape[1])
        cfg = (
            n_src // 2,
            n_x,
            n_tgt // n_x,
            eps,
            math.log2(source_latents.shape[0]),
            math.log2(target_latents.shape[0]),
        )
        return jax.shard_map(
            functools.partial(local, cfg),
            mesh=mesh,
            in_specs=(P("src", None), P("tgt", None)),
            out_specs=(P("src", "tgt"), P("src"), P("tgt")),
            check_vma=False,
        )(source_latents, target_latents)

    return whole
```

time: 688 us -> 80.7 us (0.12)
  blocking collectives: 563 us -> 0 us
  waiting for transfers between devices: 95.4 us -> 0 us
  Pallas kernels: 0 us -> 75.2 us
  between operations: 14.1 us -> 0.65 us
  other arithmetic: 9.24 us -> 0.64 us
    pmax x7 -> x0, blocking collectives: 312 us -> none  [the longest x3 187 us: collapse_source_axis(): top_score = lax.pmax(local_peak, 'src')]
    psum x7 -> x0, blocking collectives: 251 us -> none  [the longest x3 137 us: collapse_source_axis(): lax.psum(jnp.sum(jnp.exp(kernel_exponent_array - top_score[None, :]), axi...]
    reduce_scatter x1 -> x0, waiting for transfers between devices: 95.3 us -> none  [local(): lax.psum_scatter(partial_sums.astype(jnp.bfloat16), 'tgt', scatter_dimens...]
    pallas_call x0 -> x1, Pallas kernels: none -> 75.2 us  [local(): pl.pallas_call(functools.partial(kernel, cfg), out_shape=(jax.ShapeDtypeS...]
    reduce_sum x9 -> x0, other arithmetic: 7.45 us -> none  [the longest x4 2.26 us: collapse_target_axis(): jnp.sum(jnp.exp(kernel_exponent_array - top_score[:, None]), axis=1)]
  transfers between devices with their start and end apart: 1 -> 0, of which waited for: 1 -> 0; matrix products, arithmetic and copies ran while one was open for 0% -> 0% of each run, Pallas kernels for 0% -> 0%
where the time goes in v1:
time: 80.7 us; the launch traced here: 80.5 us
  Pallas kernels  75.2 us (93%)
  local copies, waits for them, and re-layouts  3.98 us (5%)
    pallas_call x1, Pallas kernels, local(): pl.pallas_call(functools.partial(kernel, cfg), out_shape=(jax.ShapeDtypeS...  75.2 us
    unnamed x6, local copies, waits for them, and re-layouts  3.98 us

profile of v1, /device:TPU:1, one launch (start us, length us, event | category | flops | bytes accessed | tf_op | source)
XLA Modules:
  0.0 80.5 jit_solution(415091055156551477)
XLA Ops:
  0.6 0.0 copy-start
  0.6 1.6 %copy-done = bf16[1024,1024]{1,0:T(8,128)(2,1)S(1)} copy-done((bf16[1024,1024]{1,0:T(8,128)(2,1)S(1)}, bf16[1024,1024]{1,0:T(8,128)(2,1)}, u32[]{:S(2)}) %copy-start) | copy-done | bytes 2097176
  2.2 0.0 copy-start.1
  2.2 1.2 %copy-done.1 = bf16[512,1024]{1,0:T(8,128)(2,1)S(1)} copy-done((bf16[512,1024]{1,0:T(8,128)(2,1)S(1)}, bf16[512,1024]{1,0:T(8,128)(2,1)}, u32[]{:S(2)}) %copy-start.1) | copy-done | bytes 1048600
  3.4 75.2 %transport.1 = (f32[64,512]{1,0:T(8,128)S(1)}, f32[4,128]{1,0:T(4,128)S(1)}, f32[8,128]{1,0:T(8,128)S(1)}) custom-call(bf16[512,1024]{1,0:T(8,128)(2,1)S(1)} %copy-done.1, bf16[1024,1024]{1,0:T(8,128)(2,1)S(1)} %copy-done), custom_call_target="tpu_custom_call" | custom-call | tf_op jit(solution)/shard_map/transport/pallas_call | solution.py:344
  78.7 0.6 convert_bitcast_fusion
  79.3 0.6 copy.7
  79.9 0.6 copy.8
Async XLA Ops:
  0.6 1.6 %copy-start = (bf16[1024,1024]{1,0:T(8,128)(2,1)S(1)}, bf16[1024,1024]{1,0:T(8,128)(2,1)}, u32[]{:S(2)}) copy-start(bf16[1024,1024]{1,0:T(8,128)(2,1)} %tgt_hbm.1) | copy-start | bytes 6291460
  2.2 1.2 %copy-start.1 = (bf16[512,1024]{1,0:T(8,128)(2,1)S(1)}, bf16[512,1024]{1,0:T(8,128)(2,1)}, u32[]{:S(2)}) copy-start(bf16[512,1024]{1,0:T(8,128)(2,1)} %src_hbm.1) | copy-start | bytes 3145732

commit v2 on v1

--- a/solution.py
+++ b/solution.py
@@ -9,6 +9,8 @@
 from jax.sharding import PartitionSpec as P
 
 ITERS = 3
+QUARTERS = 4
+CHUNKS = 2
 LOG2E = math.log2(math.e)
 LANES = 128
 F32 = jnp.float32
@@ -51,17 +53,20 @@
     b_t,
     scores,
     part,
+    mass,
     column,
     weights,
     sums,
-    arrived,
+    first_in,
+    second_out,
+    second_in,
     h_ref,
     u_ref,
     ss_ref,
     tt_ref,
     peak_ref,
     mass_ref,
-    own_lse,
+    own_scale,
     t_send,
     t_recv,
     c_send,
@@ -77,6 +82,8 @@
     z_rsem,
     m_ssem,
     m_rsem,
+    n_ssem,
+    n_rsem,
 ):
     n_z, n_x, n_y, eps, log2_rows, log2_cols = cfg
     rows, depth = a.shape
@@ -85,7 +92,8 @@
     s_me, t_me = lax.axis_index("src"), lax.axis_index("tgt")
     z_me, core_me = s_me // 2, s_me % 2
     x_me, y_me = t_me // n_y, t_me % n_y
-    feats = depth // (n_x * n_y)
+    half = depth // (n_x * n_y) // 2
+    chunk = rows // CHUNKS
 
     z_peers = []
     for k in sorted(range(1, n_z), key=lambda k: -ring_distance(k, n_z)):
@@ -106,16 +114,20 @@
             barrier, inc=1, device_id=peer, device_id_type=pl.DeviceIdType.MESH
         )
 
-    quarter = cols // 4
-    loads = [pltpu.make_async_copy(src_hbm, a, load_sem.at[4])]
-    for q in range(4):
+    quarter = cols // QUARTERS
+    loads = [pltpu.make_async_copy(src_hbm, a, load_sem.at[QUARTERS])]
+    for q in range(QUARTERS):
         piece = pl.ds(q * quarter, quarter)
         loads.append(pltpu.make_async_copy(tgt_hbm.at[piece], b.at[piece], load_sem.at[q]))
     for copy in loads:
         copy.start()
-    loads[0].wait()
-    for q in range(4):
+    for q in range(QUARTERS):
         loads[1 + q].wait()
+        blocks = range(q * quarter // LANES, (q + 1) * quarter // LANES)
+        for c in blocks:
+            square_sums(b, c * LANES, tt_ref, c)
+        if q == 0:
+            loads[0].wait()
         dot = lax.dot_general(
             a[...],
             b[q * quarter : (q + 1) * quarter, :],
@@ -123,9 +135,6 @@
             preferred_element_type=F32,
         )
         scores[:, q * quarter : (q + 1) * quarter] = dot * (2.0 * LOG2E / (depth * eps))
-        for k in range(quarter // LANES):
-            block = q * (quarter // LANES) + k
-            square_sums(b, block * LANES, tt_ref, block)
     h_ref[...] = tt_ref[...] * (-LOG2E / (depth * eps))
 
     def rows_pass(out_ref):
@@ -200,30 +209,36 @@
         )
         out_ref[...] = top + log2(total)
 
+    rows_pass(t_send.at[0])
+    pl.semaphore_wait(barrier, len(everyone))
+    start_rows_exchange(0)
+
+    for r in range(row_groups):
+        square_sums(a, r * LANES, ss_ref, r)
+    order = sorted(range(n_x), key=lambda d: -ring_distance(d, n_x))
+
+    def position(along):
+        return sum(jnp.where(along == e, o, 0) for o, e in enumerate(order))
+
+    def turn(block, carry):
+        at = pl.ds(pl.multiple_of(block * LANES, LANES), LANES)
+        for c in range(depth // LANES):
+            turned = b[at, c * LANES : (c + 1) * LANES].T
+            for o in range(LANES // half):
+                owner, second = divmod(c * (LANES // half) + o, 2)
+                ox, oy = owner // n_y, owner % n_y
+                if second:
+                    row = position((oy - y_me + n_y) % n_y) * (2 * n_y) + n_y + ox
+                else:
+                    row = position((ox - x_me + n_x) % n_x) * (2 * n_y) + oy
+                b_t[pl.ds(pl.multiple_of(row * half, half), half), at] = turned[
+                    o * half : (o + 1) * half
+                ]
+        return carry
+
+    lax.fori_loop(0, col_groups, turn, 0)
+
     def sweep(i, carry):
-        rows_pass(t_send.at[i])
-
-        @pl.when(i == 0)
-        def _():
-            pl.semaphore_wait(barrier, len(everyone))
-
-        start_rows_exchange(i)
-
-        @pl.when(i == 0)
-        def _():
-            for r in range(row_groups):
-                square_sums(a, r * LANES, ss_ref, r)
-
-            def turn(block, carry):
-                at = pl.ds(pl.multiple_of(block * LANES, LANES), LANES)
-                for c in range(depth // LANES):
-                    b_t[c * LANES : (c + 1) * LANES, at] = b[
-                        at, c * LANES : (c + 1) * LANES
-                    ].T
-                return carry
-
-            lax.fori_loop(0, col_groups, turn, 0)
-
         wait_bytes(t_recv.at[i], t_rsem.at[i])
         u_ref[...] = -log2_cols - combine(
             [t_send[i]] + [t_recv[i, k] for k in range(len(steps))]
@@ -254,12 +269,12 @@
         h_ref[...] = -log2_rows - combine(
             [z_send[i]] + [z_recv[i, k] for k in range(len(z_peers))]
         )
+        rows_pass(t_send.at[i + 1])
+        start_rows_exchange(i + 1)
         return carry
 
     lax.fori_loop(0, ITERS, sweep, 0)
 
-    rows_pass(t_send.at[ITERS])
-    start_rows_exchange(ITERS)
     to_column(t_send.at[ITERS])
     shift = [
         jnp.broadcast_to(h_ref[c : c + 1, :], (16, LANES)) for c in range(col_groups)
@@ -274,61 +289,103 @@
                 weights[at, c * LANES : (c + 1) * LANES] = jnp.exp2(v - level).astype(BF16)
         return carry
 
-    lax.fori_loop(0, rows // 32, some_weights, 0)
-
-    per_x = n_y * feats
-    for dx in sorted(range(n_x), key=lambda d: -ring_distance(d, n_x)):
-        start = pl.multiple_of(((x_me + dx) % n_x) * per_x, per_x)
-        dot = lax.dot_general(
-            b_t[pl.ds(start, per_x), :],
-            weights[...],
-            NT_DIMS,
-            preferred_element_type=F32,
-        )
-        sums[pl.ds(start, per_x), :] = dot.astype(BF16)
-        for k, step in enumerate(steps):
-            if step[0] == dx:
-                pltpu.make_async_remote_copy(
-                    src_ref=sums.at[
-                        pl.ds(pl.multiple_of(t_index[k] * feats, feats), feats)
-                    ],
-                    dst_ref=arrived.at[k],
-                    send_sem=m_ssem.at[k],
-                    recv_sem=m_rsem.at[k],
-                    device_id={"src": s_me, "tgt": t_index[k]},
-                    device_id_type=pl.DeviceIdType.MESH,
-                ).start()
+    band = n_y * half
+
+    def plane_peer(kind, step):
+        if kind == 0:
+            return {"src": s_me, "tgt": ((x_me + step) % n_x) * n_y + y_me}
+        return {"src": s_me, "tgt": x_me * n_y + (y_me + step) % n_y}
+
+    for n in range(CHUNKS):
+        per = rows // 32 // CHUNKS
+        lax.fori_loop(n * per, (n + 1) * per, some_weights, 0)
+        for o in range(0, n_x, 2):
+            at = pl.ds(o * 2 * band, 4 * band)
+            dot = lax.dot_general(
+                b_t[at, :],
+                weights[n * chunk : (n + 1) * chunk, :],
+                NT_DIMS,
+                preferred_element_type=F32,
+            )
+            sums[n, at, :] = dot.astype(BF16)
+            for p in (o, o + 1):
+                for kind in range(2):
+                    if order[p]:
+                        pltpu.make_async_remote_copy(
+                            src_ref=sums.at[n, pl.ds((2 * p + kind) * band, band)],
+                            dst_ref=first_in.at[n, kind, order[p] - 1],
+                            send_sem=m_ssem.at[n],
+                            recv_sem=m_rsem.at[n],
+                            device_id=plane_peer(kind, order[p]),
+                            device_id_type=pl.DeviceIdType.MESH,
+                        ).start()
 
     f_ref[...] = ss_ref[...] * (1.0 / depth) + u_ref[...] * (eps / LOG2E)
     g_ref[...] = tt_ref[...] * (1.0 / depth) + h_ref[...] * (eps / LOG2E)
 
     wait_bytes(t_recv.at[ITERS], t_rsem.at[ITERS])
     level = combine([t_send[ITERS]] + [t_recv[ITERS, k] for k in range(len(steps))])
-    own_lse[...] = jnp.exp2(t_send[ITERS] - level)
-    for k in range(len(steps)):
-        t_recv[ITERS, k] = jnp.exp2(t_recv[ITERS, k] - level)
-    mine = pl.ds(pl.multiple_of(t_me * feats, feats), feats)
-    for r in range(row_groups):
-        lane = slice(r * LANES, (r + 1) * LANES)
-        moved_ref[:, lane] = sums[mine, lane].astype(F32) * own_lse[r : r + 1, :]
-    for k in sorted(
-        range(len(steps)),
-        key=lambda k: ring_distance(steps[k][0], n_x) + ring_distance(steps[k][1], n_y),
-    ):
-        wait_bytes(arrived.at[k], m_rsem.at[k])
-        for r in range(row_groups):
-            lane = slice(r * LANES, (r + 1) * LANES)
-            moved_ref[:, lane] += (
-                arrived[k, :, lane].astype(F32) * t_recv[ITERS, k, r : r + 1, :]
-            )
+    own_scale[...] = jnp.exp2(t_send[ITERS] - level)
+    along = [[steps.index((d, 0)) for d in range(1, n_x)], [steps.index((0, d)) for d in range(1, n_y)]]
+    for line in along:
+        for k in line:
+            t_recv[ITERS, k] = jnp.exp2(t_recv[ITERS, k] - level)
+
+    own = order.index(0)
+    lanes = [slice(r * LANES, (r + 1) * LANES) for r in range(chunk // LANES)]
+    for n in range(CHUNKS):
+        wait_bytes(first_in.at[n], m_rsem.at[n])
+        for kind in range(2):
+            for r, lane in enumerate(lanes):
+                g = n * (chunk // LANES) + r
+                at = pl.ds((2 * own + kind) * band, band)
+                total = sums[n, at, lane].astype(F32) * own_scale[g : g + 1, :]
+                for j, k in enumerate(along[kind]):
+                    total += first_in[n, kind, j, :, lane].astype(F32) * t_recv[ITERS, k, g : g + 1, :]
+                second_out[n, kind, :, lane] = total.astype(BF16)
+            for step in order:
+                if step:
+                    to = (y_me + step) % n_y if kind == 0 else (x_me + step) % n_x
+                    pltpu.make_async_remote_copy(
+                        src_ref=second_out.at[n, kind, pl.ds(pl.multiple_of(to * half, half), half)],
+                        dst_ref=second_in.at[n, kind, step - 1],
+                        send_sem=n_ssem.at[n],
+                        recv_sem=n_rsem.at[n],
+                        device_id=plane_peer(1 - kind, step),
+                        device_id_type=pl.DeviceIdType.MESH,
+                    ).start()
+    for n in range(CHUNKS):
+        wait_bytes(second_in.at[n], n_rsem.at[n])
+        for kind in range(2):
+            me = y_me if kind == 0 else x_me
+            mine = pl.ds(pl.multiple_of(me * half, half), half)
+            for r, lane in enumerate(lanes):
+                total = second_out[n, kind, mine, lane].astype(F32)
+                for j in range(n_x - 1):
+                    total += second_in[n, kind, j, :, lane].astype(F32)
+                at = n * chunk + r * LANES
+                moved_ref[kind * half : (kind + 1) * half, at : at + LANES] = total.astype(BF16)
 
     for i in range(ITERS):
         wait_bytes(c_send.at[i], c_ssem.at[i])
         wait_bytes(z_recv.at[i], z_ssem.at[i])
     for i in range(ITERS + 1):
         wait_bytes(t_recv.at[i], t_ssem.at[i])
-    for k in range(len(steps)):
-        wait_bytes(arrived.at[k], m_ssem.at[k])
+    for n in range(CHUNKS):
+        wait_bytes(first_in.at[n], m_ssem.at[n])
+        wait_bytes(second_in.at[n], n_ssem.at[n])
+
+
+def hand_out(moved_ref, f_ref, g_ref, *outs_and_sem):
+    *outs, sem = outs_and_sem
+    copies = [
+        pltpu.make_async_copy(ref, out, sem.at[k])
+        for k, (ref, out) in enumerate(zip((moved_ref, f_ref, g_ref), outs))
+    ]
+    for copy in copies:
+        copy.start()
+    for copy in copies:
+        copy.wait()
 
 
 def local(cfg, source_latents, target_latents):
@@ -339,15 +396,18 @@
     row_groups, col_groups = rows // LANES, cols // LANES
     t_peers, z_peers = n_x * n_y - 1, n_z - 1
     vmem = pl.BlockSpec(memory_space=pltpu.VMEM)
-    hbm = pl.BlockSpec(memory_space=pl.ANY)
+    hbm = pl.BlockSpec(memory_space=pltpu.HBM)
+    anywhere = pl.BlockSpec(memory_space=pl.ANY)
     dma = pltpu.SemaphoreType.DMA
-    moved, f, g = pl.pallas_call(
+    chunk, half, band = rows // CHUNKS, feats // 2, n_y * feats // 2
+    shapes = (
+        jax.ShapeDtypeStruct((feats, rows), BF16),
+        jax.ShapeDtypeStruct((row_groups, LANES), F32),
+        jax.ShapeDtypeStruct((col_groups, LANES), F32),
+    )
+    results = pl.pallas_call(
         functools.partial(kernel, cfg),
-        out_shape=(
-            jax.ShapeDtypeStruct((feats, rows), F32),
-            jax.ShapeDtypeStruct((row_groups, LANES), F32),
-            jax.ShapeDtypeStruct((col_groups, LANES), F32),
-        ),
+        out_shape=shapes,
         in_specs=[hbm, hbm],
         out_specs=(vmem, vmem, vmem),
         scratch_shapes=[
@@ -357,9 +417,12 @@
             pltpu.VMEM((rows, cols), F32),
             pltpu.VMEM((rows, LANES), F32),
             pltpu.VMEM((rows, LANES), F32),
+            pltpu.VMEM((rows, LANES), F32),
             pltpu.VMEM((rows, cols), BF16),
-            pltpu.VMEM((depth, rows), BF16),
-            pltpu.VMEM((t_peers, feats, rows), BF16),
+            pltpu.VMEM((CHUNKS, depth, chunk), BF16),
+            pltpu.VMEM((CHUNKS, 2, n_x - 1, band, chunk), BF16),
+            pltpu.VMEM((CHUNKS, 2, band, chunk), BF16),
+            pltpu.VMEM((CHUNKS, 2, n_x - 1, half, chunk), BF16),
             pltpu.VMEM((col_groups, LANES), F32),
             pltpu.VMEM((row_groups, LANES), F32),
             pltpu.VMEM((row_groups, LANES), F32),
@@ -373,22 +436,32 @@
             pltpu.VMEM((ITERS, col_groups, LANES), F32),
             pltpu.VMEM((ITERS, col_groups, LANES), F32),
             pltpu.VMEM((ITERS, z_peers, col_groups, LANES), F32),
-            dma((5,)),
+            dma((QUARTERS + 1,)),
             dma((ITERS + 1,)),
             dma((ITERS + 1,)),
             dma((ITERS,)),
             dma((ITERS,)),
             dma((ITERS,)),
             dma((ITERS,)),
-            dma((t_peers,)),
-            dma((t_peers,)),
+            dma((CHUNKS,)),
+            dma((CHUNKS,)),
+            dma((CHUNKS,)),
+            dma((CHUNKS,)),
         ],
         compiler_params=pltpu.CompilerParams(
-            collective_id=0, has_side_effects=True, vmem_limit_bytes=40 << 20
+            collective_id=0, has_side_effects=True, vmem_limit_bytes=213 << 18
         ),
         name="transport",
     )(source_latents, target_latents)
-    return moved.T.astype(BF16), f.reshape(rows), g.reshape(cols)
+    moved, f, g = pl.pallas_call(
+        hand_out,
+        out_shape=shapes,
+        in_specs=[anywhere] * 3,
+        out_specs=(anywhere,) * 3,
+        scratch_shapes=[dma((3,))],
+        name="hand_out",
+    )(*results)
+    return moved.T, f.reshape(rows), g.reshape(cols)
 
 
 def solution(mesh):

time: 80.7 us -> 78.1 us (0.968)
  local copies, waits for them, and re-layouts: 3.98 us -> 1.77 us
    unnamed x6, local copies, waits for them, and re-layouts: 3.98 us -> 1.77 us
    pallas_call x1 -> x2, Pallas kernels: 75.2 us -> 75.6 us  [the longest x1 72.3 us: local(): pl.pallas_call(functools.partial(kernel, cfg), out_shape=shapes, in_specs...]
where the time goes in v2:
time: 78.1 us; the launch traced here: 78 us
  Pallas kernels  75.6 us (97%)
  local copies, waits for them, and re-layouts  1.77 us (2%)
    pallas_call x1, Pallas kernels, local(): pl.pallas_call(functools.partial(kernel, cfg), out_shape=shapes, in_specs...  72.3 us
    pallas_call x1, Pallas kernels, local(): pl.pallas_call(hand_out, out_shape=shapes, in_specs=[anywhere] * 3, out_s...  3.3 us
    unnamed x6, local copies, waits for them, and re-layouts  1.77 us

profile of v2, /device:TPU:1, one launch (start us, length us, event | category | flops | bytes accessed | tf_op | source)
XLA Modules:
  0.0 78.0 jit_solution(1919995518217764164)
XLA Ops:
  0.6 72.3 %transport.1 = (bf16[64,512]{1,0:T(8,128)(2,1)S(1)}, f32[4,128]{1,0:T(4,128)S(1)}, f32[8,128]{1,0:T(8,128)S(1)}) custom-call(bf16[512,1024]{1,0:T(8,128)(2,1)} %src_hbm.1, bf16[1024,1024]{1,0:T(8,128)(2,1)} %tgt_hbm.1), custom_call_target="tpu_custom_call" | custom-call | tf_op jit(solution)/shard_map/transport/pallas_call | solution.py:408
  72.9 0.0 copy-start
  72.9 0.6 copy-done
  73.5 0.0 copy-start.1
  73.5 0.6 copy-done.1
  74.1 0.0 copy-start.2
  74.1 0.6 copy-done.2
  74.7 3.3 %hand_out.1 = (bf16[64,512]{1,0:T(8,128)(2,1)}, f32[4,128]{1,0:T(4,128)}, f32[8,128]{1,0:T(8,128)}) custom-call(bf16[64,512]{1,0:T(8,128)(2,1)} %copy-done, f32[4,128]{1,0:T(4,128)} %copy-done.2, f32[8,128]{1,0:T(8,128)} %copy-done.1), custom_call_target="tpu_custom_call" | custom-call | tf_op jit(solution)/shard_map/hand_out/pallas_call | solution.py:456
Async XLA Ops:
  72.9 0.6 copy-start
  73.5 0.6 copy-start.1
  74.1 0.6 copy-start.2

commit v3 on v2

--- a/solution.py
+++ b/solution.py
@@ -9,7 +9,7 @@
 from jax.sharding import PartitionSpec as P
 
 ITERS = 3
-QUARTERS = 4
+LOADS = 2
 CHUNKS = 2
 LOG2E = math.log2(math.e)
 LANES = 128
@@ -53,7 +53,6 @@
     b_t,
     scores,
     part,
-    mass,
     column,
     weights,
     sums,
@@ -114,27 +113,27 @@
             barrier, inc=1, device_id=peer, device_id_type=pl.DeviceIdType.MESH
         )
 
-    quarter = cols // QUARTERS
-    loads = [pltpu.make_async_copy(src_hbm, a, load_sem.at[QUARTERS])]
-    for q in range(QUARTERS):
-        piece = pl.ds(q * quarter, quarter)
+    share = cols // LOADS
+    loads = [pltpu.make_async_copy(src_hbm, a, load_sem.at[LOADS])]
+    for q in range(LOADS):
+        piece = pl.ds(q * share, share)
         loads.append(pltpu.make_async_copy(tgt_hbm.at[piece], b.at[piece], load_sem.at[q]))
     for copy in loads:
         copy.start()
-    for q in range(QUARTERS):
+    for q in range(LOADS):
         loads[1 + q].wait()
-        blocks = range(q * quarter // LANES, (q + 1) * quarter // LANES)
+        blocks = range(q * share // LANES, (q + 1) * share // LANES)
         for c in blocks:
             square_sums(b, c * LANES, tt_ref, c)
         if q == 0:
             loads[0].wait()
         dot = lax.dot_general(
             a[...],
-            b[q * quarter : (q + 1) * quarter, :],
+            b[q * share : (q + 1) * share, :],
             NT_DIMS,
             preferred_element_type=F32,
         )
-        scores[:, q * quarter : (q + 1) * quarter] = dot * (2.0 * LOG2E / (depth * eps))
+        scores[:, q * share : (q + 1) * share] = dot * (2.0 * LOG2E / (depth * eps))
     h_ref[...] = tt_ref[...] * (-LOG2E / (depth * eps))
 
     def rows_pass(out_ref):
@@ -142,17 +141,12 @@
             jnp.broadcast_to(h_ref[c : c + 1, :], (8, LANES)) for c in range(col_groups)
         ]
 
-        def some_rows(block, carry):
-            for k in range(4):
-                at = pl.ds(pl.multiple_of(block * 32 + k * 8, 8), 8)
-                v = [
-                    scores[at, c * LANES : (c + 1) * LANES] + shift[c]
-                    for c in range(col_groups)
-                ]
-                part[at, :] = combine(v)
-            return carry
-
-        lax.fori_loop(0, rows // 32, some_rows, 0)
+        for k in range(0, rows, 8):
+            v = [
+                scores[k : k + 8, c * LANES : (c + 1) * LANES] + shift[c]
+                for c in range(col_groups)
+            ]
+            part[k : k + 8, :] = combine(v)
         for r in range(row_groups):
             x = part[r * LANES : (r + 1) * LANES, :].T
             top = jnp.max(x, axis=0, keepdims=True)
@@ -197,7 +191,7 @@
                 tops[c] = top
             return tuple(tops + totals)
 
-        done = lax.fori_loop(0, rows // 64, some_rows, start)
+        done = lax.fori_loop(0, rows // 64, some_rows, start, unroll=4)
         for c in range(col_groups):
             peak_ref[c * 8 : (c + 1) * 8, :] = done[c]
             mass_ref[c * 8 : (c + 1) * 8, :] = done[col_groups + c]
@@ -280,14 +274,13 @@
         jnp.broadcast_to(h_ref[c : c + 1, :], (16, LANES)) for c in range(col_groups)
     ]
 
-    def some_weights(block, carry):
-        for k in range(2):
-            at = pl.ds(pl.multiple_of(block * 32 + k * 16, 16), 16)
+    def weigh(begin, end):
+        for k in range(begin, end, 16):
+            at = slice(k, k + 16)
             level = column[at, :]
             for c in range(col_groups):
                 v = scores[at, c * LANES : (c + 1) * LANES] + shift[c]
                 weights[at, c * LANES : (c + 1) * LANES] = jnp.exp2(v - level).astype(BF16)
-        return carry
 
     band = n_y * half
 
@@ -297,8 +290,7 @@
         return {"src": s_me, "tgt": x_me * n_y + (y_me + step) % n_y}
 
     for n in range(CHUNKS):
-        per = rows // 32 // CHUNKS
-        lax.fori_loop(n * per, (n + 1) * per, some_weights, 0)
+        weigh(n * chunk, (n + 1) * chunk)
         for o in range(0, n_x, 2):
             at = pl.ds(o * 2 * band, 4 * band)
             dot = lax.dot_general(
@@ -376,18 +368,6 @@
         wait_bytes(second_in.at[n], n_ssem.at[n])
 
 
-def hand_out(moved_ref, f_ref, g_ref, *outs_and_sem):
-    *outs, sem = outs_and_sem
-    copies = [
-        pltpu.make_async_copy(ref, out, sem.at[k])
-        for k, (ref, out) in enumerate(zip((moved_ref, f_ref, g_ref), outs))
-    ]
-    for copy in copies:
-        copy.start()
-    for copy in copies:
-        copy.wait()
-
-
 def local(cfg, source_latents, target_latents):
     n_z, n_x, n_y = cfg[:3]
     rows, depth = source_latents.shape
@@ -397,7 +377,6 @@
     t_peers, z_peers = n_x * n_y - 1, n_z - 1
     vmem = pl.BlockSpec(memory_space=pltpu.VMEM)
     hbm = pl.BlockSpec(memory_space=pltpu.HBM)
-    anywhere = pl.BlockSpec(memory_space=pl.ANY)
     dma = pltpu.SemaphoreType.DMA
     chunk, half, band = rows // CHUNKS, feats // 2, n_y * feats // 2
     shapes = (
@@ -405,7 +384,7 @@
         jax.ShapeDtypeStruct((row_groups, LANES), F32),
         jax.ShapeDtypeStruct((col_groups, LANES), F32),
     )
-    results = pl.pallas_call(
+    moved, f, g = pl.pallas_call(
         functools.partial(kernel, cfg),
         out_shape=shapes,
         in_specs=[hbm, hbm],
@@ -415,7 +394,6 @@
             pltpu.VMEM((cols, depth), BF16),
             pltpu.VMEM((depth, cols), BF16),
             pltpu.VMEM((rows, cols), F32),
-            pltpu.VMEM((rows, LANES), F32),
             pltpu.VMEM((rows, LANES), F32),
             pltpu.VMEM((rows, LANES), F32),
             pltpu.VMEM((rows, cols), BF16),
@@ -436,7 +414,7 @@
             pltpu.VMEM((ITERS, col_groups, LANES), F32),
             pltpu.VMEM((ITERS, col_groups, LANES), F32),
             pltpu.VMEM((ITERS, z_peers, col_groups, LANES), F32),
-            dma((QUARTERS + 1,)),
+            dma((LOADS + 1,)),
             dma((ITERS + 1,)),
             dma((ITERS + 1,)),
             dma((ITERS,)),
@@ -453,14 +431,6 @@
         ),
         name="transport",
     )(source_latents, target_latents)
-    moved, f, g = pl.pallas_call(
-        hand_out,
-        out_shape=shapes,
-        in_specs=[anywhere] * 3,
-        out_specs=(anywhere,) * 3,
-        scratch_shapes=[dma((3,))],
-        name="hand_out",
-    )(*results)
     return moved.T, f.reshape(rows), g.reshape(cols)
 
 

time: 78.1 us -> 72 us (0.922)
  Pallas kernels: 75.6 us -> 69.4 us
    pallas_call x1 -> x0, Pallas kernels: 3.3 us -> none  [local(): pl.pallas_call(hand_out, out_shape=shapes, in_specs=[anywhere] * 3, out_s...]
    pallas_call x1, Pallas kernels: 72.3 us -> 69.4 us  [local(): pl.pallas_call(functools.partial(kernel, cfg), out_shape=shapes, in_specs...]
    unnamed x6 -> x3, local copies, waits for them, and re-layouts: 1.77 us -> 1.8 us
where the time goes in v3:
time: 72 us; the launch traced here: 71.8 us
  Pallas kernels  69.4 us (96%)
  local copies, waits for them, and re-layouts  1.8 us (2%)
    pallas_call x1, Pallas kernels, local(): pl.pallas_call(functools.partial(kernel, cfg), out_shape=shapes, in_specs...  69.4 us
    unnamed x3, local copies, waits for them, and re-layouts  1.8 us

profile of v3, /device:TPU:1, one launch (start us, length us, event | category | flops | bytes accessed | tf_op | source)
XLA Modules:
  0.0 71.8 jit_solution(3471490620481991497)
XLA Ops:
  0.6 69.4 %transport.1 = (bf16[64,512]{1,0:T(8,128)(2,1)S(1)}, f32[4,128]{1,0:T(4,128)S(1)}, f32[8,128]{1,0:T(8,128)S(1)}) custom-call(bf16[512,1024]{1,0:T(8,128)(2,1)} %src_hbm.1, bf16[1024,1024]{1,0:T(8,128)(2,1)} %tgt_hbm.1), custom_call_target="tpu_custom_call" | custom-call | tf_op jit(solution)/shard_map/transport/pallas_call | solution.py:387
  70.0 0.6 copy.8
  70.7 0.6 copy.9
  71.2 0.6 copy.10

commit v4 on v3

--- a/solution.py
+++ b/solution.py
@@ -11,6 +11,7 @@
 ITERS = 3
 LOADS = 2
 CHUNKS = 2
+LEAD = 0
 LOG2E = math.log2(math.e)
 LANES = 128
 F32 = jnp.float32
@@ -26,10 +27,16 @@
     return jnp.log(x) * LOG2E
 
 
+def tree(op, parts):
+    while len(parts) > 1:
+        paired = [op(p, q) for p, q in zip(parts[::2], parts[1::2])]
+        parts = paired + parts[len(parts) - len(parts) % 2 :]
+    return parts[0]
+
+
 def combine(parts):
-    top = functools.reduce(jnp.maximum, parts)
-    total = functools.reduce(jnp.add, [jnp.exp2(p - top) for p in parts])
-    return top + log2(total)
+    top = tree(jnp.maximum, parts)
+    return top + log2(tree(jnp.add, [jnp.exp2(p - top) for p in parts]))
 
 
 def square_sums(block_ref, start, out_ref, row):
@@ -70,7 +77,6 @@
     t_recv,
     c_send,
     c_recv,
-    z_send,
     z_recv,
     load_sem,
     t_ssem,
@@ -94,9 +100,11 @@
     half = depth // (n_x * n_y) // 2
     chunk = rows // CHUNKS
 
-    z_peers = []
-    for k in sorted(range(1, n_z), key=lambda k: -ring_distance(k, n_z)):
-        z_peers.append({"src": ((z_me + k) % n_z) * 2 + core_me, "tgt": t_me})
+    z_steps = sorted(range(1, n_z), key=lambda k: -ring_distance(k, n_z))
+
+    def z_peer(k, core):
+        return {"src": ((z_me + k) % n_z) * 2 + core, "tgt": t_me}
+
     sibling = {"src": z_me * 2 + (1 - core_me), "tgt": t_me}
     steps = [(dx, dy) for dx in range(n_x) for dy in range(n_y) if dx or dy]
     steps.sort(key=lambda d: (-ring_distance(d[0], n_x), -ring_distance(d[1], n_y)))
@@ -106,13 +114,6 @@
         key=lambda k: -ring_distance(steps[k][0], n_x) - ring_distance(steps[k][1], n_y),
     )
 
-    barrier = pltpu.get_barrier_semaphore()
-    everyone = z_peers + [{"src": s_me, "tgt": t_index[k]} for k in far] + [sibling]
-    for peer in everyone:
-        pl.semaphore_signal(
-            barrier, inc=1, device_id=peer, device_id_type=pl.DeviceIdType.MESH
-        )
-
     share = cols // LOADS
     loads = [pltpu.make_async_copy(src_hbm, a, load_sem.at[LOADS])]
     for q in range(LOADS):
@@ -120,6 +121,16 @@
         loads.append(pltpu.make_async_copy(tgt_hbm.at[piece], b.at[piece], load_sem.at[q]))
     for copy in loads:
         copy.start()
+
+    leads = core_me == LEAD
+    barrier = pltpu.get_barrier_semaphore()
+    everyone = [z_peer(k, LEAD) for k in z_steps]
+    everyone += [{"src": s_me, "tgt": t_index[k]} for k in far] + [sibling]
+    for peer in everyone:
+        pl.semaphore_signal(
+            barrier, inc=1, device_id=peer, device_id_type=pl.DeviceIdType.MESH
+        )
+
     for q in range(LOADS):
         loads[1 + q].wait()
         blocks = range(q * share // LANES, (q + 1) * share // LANES)
@@ -185,8 +196,8 @@
             u = [column[p, :] for p in at]
             for c in range(col_groups):
                 v = [scores[p, c * LANES : (c + 1) * LANES] + w for p, w in zip(at, u)]
-                top = functools.reduce(jnp.maximum, v + [tops[c]])
-                mass = functools.reduce(jnp.add, [jnp.exp2(p - top) for p in v])
+                top = jnp.maximum(tree(jnp.maximum, v), tops[c])
+                mass = tree(jnp.add, [jnp.exp2(p - top) for p in v])
                 totals[c] = totals[c] * jnp.exp2(tops[c] - top) + mass
                 tops[c] = top
             return tuple(tops + totals)
@@ -197,14 +208,20 @@
             mass_ref[c * 8 : (c + 1) * 8, :] = done[col_groups + c]
         peaks = [peak_ref[pl.ds(r, col_groups, stride=8), :] for r in range(8)]
         masses = [mass_ref[pl.ds(r, col_groups, stride=8), :] for r in range(8)]
-        top = functools.reduce(jnp.maximum, peaks)
-        total = functools.reduce(
-            jnp.add, [m * jnp.exp2(p - top) for p, m in zip(peaks, masses)]
-        )
+        top = tree(jnp.maximum, peaks)
+        total = tree(jnp.add, [m * jnp.exp2(p - top) for p, m in zip(peaks, masses)])
         out_ref[...] = top + log2(total)
 
     rows_pass(t_send.at[0])
-    pl.semaphore_wait(barrier, len(everyone))
+
+    @pl.when(leads)
+    def _():
+        pl.semaphore_wait(barrier, len(far) + 1 + 2 * len(z_steps))
+
+    @pl.when(jnp.logical_not(leads))
+    def _():
+        pl.semaphore_wait(barrier, len(far) + 1)
+
     start_rows_exchange(0)
 
     for r in range(row_groups):
@@ -232,6 +249,8 @@
 
     lax.fori_loop(0, col_groups, turn, 0)
 
+    own_slot = n_z - 1
+
     def sweep(i, carry):
         wait_bytes(t_recv.at[i], t_rsem.at[i])
         u_ref[...] = -log2_cols - combine(
@@ -247,22 +266,34 @@
             device_id=sibling,
             device_id_type=pl.DeviceIdType.MESH,
         )
-        copy.start()
-        copy.wait_recv()
-        z_send[i] = combine([c_send[i], c_recv[i]])
-        for k, peer in enumerate(z_peers):
-            pltpu.make_async_remote_copy(
-                src_ref=z_send.at[i],
-                dst_ref=z_recv.at[i, k],
-                send_sem=z_ssem.at[i],
-                recv_sem=z_rsem.at[i],
-                device_id=peer,
-                device_id_type=pl.DeviceIdType.MESH,
-            ).start()
-        wait_bytes(z_recv.at[i], z_rsem.at[i])
-        h_ref[...] = -log2_rows - combine(
-            [z_send[i]] + [z_recv[i, k] for k in range(len(z_peers))]
-        )
+
+        @pl.when(jnp.logical_not(leads))
+        def _():
+            copy.start()
+            wait_bytes(z_recv.at[i], z_rsem.at[i])
+
+        @pl.when(leads)
+        def _():
+            copy.wait_recv()
+            z_recv[i, own_slot] = combine([c_send[i], c_recv[i]])
+
+            def send(slot, peer):
+                pltpu.make_async_remote_copy(
+                    src_ref=z_recv.at[i, own_slot],
+                    dst_ref=z_recv.at[i, slot],
+                    send_sem=z_ssem.at[i],
+                    recv_sem=z_rsem.at[i],
+                    device_id=peer,
+                    device_id_type=pl.DeviceIdType.MESH,
+                ).start()
+
+            for k in z_steps:
+                send(k - 1, z_peer(k, 1 - LEAD))
+                send(k - 1, z_peer(k, LEAD))
+            send(own_slot, sibling)
+            wait_bytes(z_recv.at[i, pl.ds(0, own_slot)], z_rsem.at[i])
+
+        h_ref[...] = -log2_rows - combine([z_recv[i, k] for k in range(n_z)])
         rows_pass(t_send.at[i + 1])
         start_rows_exchange(i + 1)
         return carry
@@ -359,8 +390,16 @@
                 moved_ref[kind * half : (kind + 1) * half, at : at + LANES] = total.astype(BF16)
 
     for i in range(ITERS):
-        wait_bytes(c_send.at[i], c_ssem.at[i])
-        wait_bytes(z_recv.at[i], z_ssem.at[i])
+
+        @pl.when(jnp.logical_not(leads))
+        def _():
+            wait_bytes(c_send.at[i], c_ssem.at[i])
+
+        @pl.when(leads)
+        def _():
+            wait_bytes(z_recv.at[i], z_ssem.at[i])
+            wait_bytes(z_recv.at[i, pl.ds(0, own_slot)], z_ssem.at[i])
+
     for i in range(ITERS + 1):
         wait_bytes(t_recv.at[i], t_ssem.at[i])
     for n in range(CHUNKS):
@@ -374,7 +413,7 @@
     cols = target_latents.shape[0]
     feats = depth // (n_x * n_y)
     row_groups, col_groups = rows // LANES, cols // LANES
-    t_peers, z_peers = n_x * n_y - 1, n_z - 1
+    t_peers = n_x * n_y - 1
     vmem = pl.BlockSpec(memory_space=pltpu.VMEM)
     hbm = pl.BlockSpec(memory_space=pltpu.HBM)
     dma = pltpu.SemaphoreType.DMA
@@ -412,8 +451,7 @@
             pltpu.VMEM((ITERS + 1, t_peers, row_groups, LANES), F32),
             pltpu.VMEM((ITERS, col_groups, LANES), F32),
             pltpu.VMEM((ITERS, col_groups, LANES), F32),
-            pltpu.VMEM((ITERS, col_groups, LANES), F32),
-            pltpu.VMEM((ITERS, z_peers, col_groups, LANES), F32),
+            pltpu.VMEM((ITERS, n_z, col_groups, LANES), F32),
             dma((LOADS + 1,)),
             dma((ITERS + 1,)),
             dma((ITERS + 1,)),

time: 72 us -> 71.2 us (0.989)
  Pallas kernels: 69.4 us -> 68.6 us
    pallas_call x1, Pallas kernels: 69.4 us -> 68.6 us  [local(): pl.pallas_call(functools.partial(kernel, cfg), out_shape=shapes, in_specs...]
where the time goes in v4:
time: 71.2 us; the launch traced here: 71.1 us
  Pallas kernels  68.6 us (96%)
  local copies, waits for them, and re-layouts  1.8 us (3%)
    pallas_call x1, Pallas kernels, local(): pl.pallas_call(functools.partial(kernel, cfg), out_shape=shapes, in_specs...  68.6 us
    unnamed x3, local copies, waits for them, and re-layouts  1.8 us

profile of v4, /device:TPU:1, one launch (start us, length us, event | category | flops | bytes accessed | tf_op | source)
XLA Modules:
  0.0 71.1 jit_solution(15037604116105315282)
XLA Ops:
  0.6 68.6 %transport.1 = (bf16[64,512]{1,0:T(8,128)(2,1)S(1)}, f32[4,128]{1,0:T(4,128)S(1)}, f32[8,128]{1,0:T(8,128)S(1)}) custom-call(bf16[512,1024]{1,0:T(8,128)(2,1)} %src_hbm.1, bf16[1024,1024]{1,0:T(8,128)(2,1)} %tgt_hbm.1), custom_call_target="tpu_custom_call" | custom-call | tf_op jit(solution)/shard_map/transport/pallas_call | solution.py:426
  69.3 0.6 copy.8
  69.9 0.6 copy.9
  70.5 0.6 copy.10

commit v5 on v4

--- a/solution.py
+++ b/solution.py
@@ -147,26 +147,26 @@
         scores[:, q * share : (q + 1) * share] = dot * (2.0 * LOG2E / (depth * eps))
     h_ref[...] = tt_ref[...] * (-LOG2E / (depth * eps))
 
-    def rows_pass(out_ref):
+    def rows_pass(out_ref, begin=0, end=rows):
         shift = [
             jnp.broadcast_to(h_ref[c : c + 1, :], (8, LANES)) for c in range(col_groups)
         ]
 
-        for k in range(0, rows, 8):
+        for k in range(begin, end, 8):
             v = [
                 scores[k : k + 8, c * LANES : (c + 1) * LANES] + shift[c]
                 for c in range(col_groups)
             ]
             part[k : k + 8, :] = combine(v)
-        for r in range(row_groups):
+        for r in range(begin // LANES, end // LANES):
             x = part[r * LANES : (r + 1) * LANES, :].T
             top = jnp.max(x, axis=0, keepdims=True)
             out_ref[r : r + 1, :] = top + log2(
                 jnp.sum(jnp.exp2(x - top), axis=0, keepdims=True)
             )
 
-    def to_column(ref):
-        for r in range(row_groups):
+    def to_column(ref, begin=0, end=rows):
+        for r in range(begin // LANES, end // LANES):
             column[r * LANES : (r + 1) * LANES, :] = jnp.broadcast_to(
                 ref[r : r + 1, :], (LANES, LANES)
             ).T
@@ -294,13 +294,16 @@
             wait_bytes(z_recv.at[i, pl.ds(0, own_slot)], z_rsem.at[i])
 
         h_ref[...] = -log2_rows - combine([z_recv[i, k] for k in range(n_z)])
-        rows_pass(t_send.at[i + 1])
-        start_rows_exchange(i + 1)
+
+        @pl.when(i < ITERS - 1)
+        def _():
+            rows_pass(t_send.at[i + 1])
+            start_rows_exchange(i + 1)
+
         return carry
 
     lax.fori_loop(0, ITERS, sweep, 0)
 
-    to_column(t_send.at[ITERS])
     shift = [
         jnp.broadcast_to(h_ref[c : c + 1, :], (16, LANES)) for c in range(col_groups)
     ]
@@ -321,6 +324,10 @@
         return {"src": s_me, "tgt": x_me * n_y + (y_me + step) % n_y}
 
     for n in range(CHUNKS):
+        rows_pass(t_send.at[ITERS], n * chunk, (n + 1) * chunk)
+        if n == CHUNKS - 1:
+            start_rows_exchange(ITERS)
+        to_column(t_send.at[ITERS], n * chunk, (n + 1) * chunk)
         weigh(n * chunk, (n + 1) * chunk)
         for o in range(0, n_x, 2):
             at = pl.ds(o * 2 * band, 4 * band)

time: 71.2 us -> 71.8 us (level)
  no operation moved by 1% of the time
where the time goes in v5:
time: 71.8 us; the launch traced here: 71.6 us
  Pallas kernels  69.2 us (96%)
  local copies, waits for them, and re-layouts  1.8 us (3%)
    pallas_call x1, Pallas kernels, local(): pl.pallas_call(functools.partial(kernel, cfg), out_shape=shapes, in_specs...  69.2 us
    unnamed x3, local copies, waits for them, and re-layouts  1.8 us

profile of v5, /device:TPU:1, one launch (start us, length us, event | category | flops | bytes accessed | tf_op | source)
XLA Modules:
  0.0 71.6 jit_solution(7843668357676480974)
XLA Ops:
  0.6 69.2 %transport.1 = (bf16[64,512]{1,0:T(8,128)(2,1)S(1)}, f32[4,128]{1,0:T(4,128)S(1)}, f32[8,128]{1,0:T(8,128)S(1)}) custom-call(bf16[512,1024]{1,0:T(8,128)(2,1)} %src_hbm.1, bf16[1024,1024]{1,0:T(8,128)(2,1)} %tgt_hbm.1), custom_call_target="tpu_custom_call" | custom-call | tf_op jit(solution)/shard_map/transport/pallas_call | solution.py:433
  69.8 0.6 copy.8
  70.5 0.6 copy.9
  71.0 0.6 copy.10

commit v6 on v4

--- a/solution.py
+++ b/solution.py
@@ -147,37 +147,41 @@
         scores[:, q * share : (q + 1) * share] = dot * (2.0 * LOG2E / (depth * eps))
     h_ref[...] = tt_ref[...] * (-LOG2E / (depth * eps))
 
-    def rows_pass(out_ref):
+    groups = chunk // LANES
+
+    def rows_pass(i, n):
         shift = [
             jnp.broadcast_to(h_ref[c : c + 1, :], (8, LANES)) for c in range(col_groups)
         ]
 
-        for k in range(0, rows, 8):
+        for k in range(n * chunk, (n + 1) * chunk, 8):
             v = [
                 scores[k : k + 8, c * LANES : (c + 1) * LANES] + shift[c]
                 for c in range(col_groups)
             ]
             part[k : k + 8, :] = combine(v)
-        for r in range(row_groups):
-            x = part[r * LANES : (r + 1) * LANES, :].T
+        for r in range(groups):
+            at = n * chunk + r * LANES
+            x = part[at : at + LANES, :].T
             top = jnp.max(x, axis=0, keepdims=True)
-            out_ref[r : r + 1, :] = top + log2(
+            t_send[i, n, r : r + 1, :] = top + log2(
                 jnp.sum(jnp.exp2(x - top), axis=0, keepdims=True)
             )
 
-    def to_column(ref):
-        for r in range(row_groups):
-            column[r * LANES : (r + 1) * LANES, :] = jnp.broadcast_to(
+    def to_column(ref, n):
+        for r in range(groups):
+            at = n * chunk + r * LANES
+            column[at : at + LANES, :] = jnp.broadcast_to(
                 ref[r : r + 1, :], (LANES, LANES)
             ).T
 
-    def start_rows_exchange(i):
+    def start_rows_exchange(i, n):
         for k in far:
             pltpu.make_async_remote_copy(
-                src_ref=t_send.at[i],
-                dst_ref=t_recv.at[i, k],
-                send_sem=t_ssem.at[i],
-                recv_sem=t_rsem.at[i],
+                src_ref=t_send.at[i, n],
+                dst_ref=t_recv.at[i, n, k],
+                send_sem=t_ssem.at[i, n],
+                recv_sem=t_rsem.at[i, n],
                 device_id={"src": s_me, "tgt": t_index[k]},
                 device_id_type=pl.DeviceIdType.MESH,
             ).start()
@@ -185,7 +189,7 @@
     def wait_bytes(ref, sem):
         pltpu.make_async_copy(ref, ref, sem).wait()
 
-    def columns_pass(out_ref):
+    def columns_pass(i, out_ref):
         shape = (8, LANES)
         low = jnp.full(shape, -3.0e38, F32)
         start = tuple([low] * col_groups + [jnp.zeros(shape, F32)] * col_groups)
@@ -202,7 +206,15 @@
                 tops[c] = top
             return tuple(tops + totals)
 
-        done = lax.fori_loop(0, rows // 64, some_rows, start, unroll=4)
+        done = start
+        for n in range(CHUNKS):
+            wait_bytes(t_recv.at[i, n], t_rsem.at[i, n])
+            u_ref[n] = -log2_cols - combine(
+                [t_send[i, n]] + [t_recv[i, n, k] for k in range(len(steps))]
+            )
+            to_column(u_ref.at[n], n)
+            per = chunk // 64
+            done = lax.fori_loop(n * per, (n + 1) * per, some_rows, done, unroll=True)
         for c in range(col_groups):
             peak_ref[c * 8 : (c + 1) * 8, :] = done[c]
             mass_ref[c * 8 : (c + 1) * 8, :] = done[col_groups + c]
@@ -212,7 +224,7 @@
         total = tree(jnp.add, [m * jnp.exp2(p - top) for p, m in zip(peaks, masses)])
         out_ref[...] = top + log2(total)
 
-    rows_pass(t_send.at[0])
+    rows_pass(0, 0)
 
     @pl.when(leads)
     def _():
@@ -222,7 +234,10 @@
     def _():
         pl.semaphore_wait(barrier, len(far) + 1)
 
-    start_rows_exchange(0)
+    start_rows_exchange(0, 0)
+    for n in range(1, CHUNKS):
+        rows_pass(0, n)
+        start_rows_exchange(0, n)
 
     for r in range(row_groups):
         square_sums(a, r * LANES, ss_ref, r)
@@ -252,12 +267,7 @@
     own_slot = n_z - 1
 
     def sweep(i, carry):
-        wait_bytes(t_recv.at[i], t_rsem.at[i])
-        u_ref[...] = -log2_cols - combine(
-            [t_send[i]] + [t_recv[i, k] for k in range(len(steps))]
-        )
-        to_column(u_ref)
-        columns_pass(c_send.at[i])
+        columns_pass(i, c_send.at[i])
         copy = pltpu.make_async_remote_copy(
             src_ref=c_send.at[i],
             dst_ref=c_recv.at[i],
@@ -294,13 +304,17 @@
             wait_bytes(z_recv.at[i, pl.ds(0, own_slot)], z_rsem.at[i])
 
         h_ref[...] = -log2_rows - combine([z_recv[i, k] for k in range(n_z)])
-        rows_pass(t_send.at[i + 1])
-        start_rows_exchange(i + 1)
+
+        @pl.when(i < ITERS - 1)
+        def _():
+            for n in range(CHUNKS):
+                rows_pass(i + 1, n)
+                start_rows_exchange(i + 1, n)
+
         return carry
 
     lax.fori_loop(0, ITERS, sweep, 0)
 
-    to_column(t_send.at[ITERS])
     shift = [
         jnp.broadcast_to(h_ref[c : c + 1, :], (16, LANES)) for c in range(col_groups)
     ]
@@ -321,6 +335,9 @@
         return {"src": s_me, "tgt": x_me * n_y + (y_me + step) % n_y}
 
     for n in range(CHUNKS):
+        rows_pass(ITERS, n)
+        start_rows_exchange(ITERS, n)
+        to_column(t_send.at[ITERS, n], n)
         weigh(n * chunk, (n + 1) * chunk)
         for o in range(0, n_x, 2):
             at = pl.ds(o * 2 * band, 4 * band)
@@ -343,16 +360,24 @@
                             device_id_type=pl.DeviceIdType.MESH,
                         ).start()
 
-    f_ref[...] = ss_ref[...] * (1.0 / depth) + u_ref[...] * (eps / LOG2E)
+    for n in range(CHUNKS):
+        at = slice(n * groups, (n + 1) * groups)
+        f_ref[at, :] = ss_ref[at, :] * (1.0 / depth) + u_ref[n] * (eps / LOG2E)
     g_ref[...] = tt_ref[...] * (1.0 / depth) + h_ref[...] * (eps / LOG2E)
 
-    wait_bytes(t_recv.at[ITERS], t_rsem.at[ITERS])
-    level = combine([t_send[ITERS]] + [t_recv[ITERS, k] for k in range(len(steps))])
-    own_scale[...] = jnp.exp2(t_send[ITERS] - level)
-    along = [[steps.index((d, 0)) for d in range(1, n_x)], [steps.index((0, d)) for d in range(1, n_y)]]
-    for line in along:
-        for k in line:
-            t_recv[ITERS, k] = jnp.exp2(t_recv[ITERS, k] - level)
+    along = [
+        [steps.index((d, 0)) for d in range(1, n_x)],
+        [steps.index((0, d)) for d in range(1, n_y)],
+    ]
+    for n in range(CHUNKS):
+        wait_bytes(t_recv.at[ITERS, n], t_rsem.at[ITERS, n])
+        level = combine(
+            [t_send[ITERS, n]] + [t_recv[ITERS, n, k] for k in range(len(steps))]
+        )
+        own_scale[n] = jnp.exp2(t_send[ITERS, n] - level)
+        for line in along:
+            for k in line:
+                t_recv[ITERS, n, k] = jnp.exp2(t_recv[ITERS, n, k] - level)
 
     own = order.index(0)
     lanes = [slice(r * LANES, (r + 1) * LANES) for r in range(chunk // LANES)]
@@ -360,11 +385,10 @@
         wait_bytes(first_in.at[n], m_rsem.at[n])
         for kind in range(2):
             for r, lane in enumerate(lanes):
-                g = n * (chunk // LANES) + r
                 at = pl.ds((2 * own + kind) * band, band)
-                total = sums[n, at, lane].astype(F32) * own_scale[g : g + 1, :]
+                total = sums[n, at, lane].astype(F32) * own_scale[n, r : r + 1, :]
                 for j, k in enumerate(along[kind]):
-                    total += first_in[n, kind, j, :, lane].astype(F32) * t_recv[ITERS, k, g : g + 1, :]
+                    total += first_in[n, kind, j, :, lane].astype(F32) * t_recv[ITERS, n, k, r : r + 1, :]
                 second_out[n, kind, :, lane] = total.astype(BF16)
             for step in order:
                 if step:
@@ -401,7 +425,8 @@
             wait_bytes(z_recv.at[i, pl.ds(0, own_slot)], z_ssem.at[i])
 
     for i in range(ITERS + 1):
-        wait_bytes(t_recv.at[i], t_ssem.at[i])
+        for n in range(CHUNKS):
+            wait_bytes(t_recv.at[i, n], t_ssem.at[i, n])
     for n in range(CHUNKS):
         wait_bytes(first_in.at[n], m_ssem.at[n])
         wait_bytes(second_in.at[n], n_ssem.at[n])
@@ -413,6 +438,7 @@
     cols = target_latents.shape[0]
     feats = depth // (n_x * n_y)
     row_groups, col_groups = rows // LANES, cols // LANES
+    groups = rows // CHUNKS // LANES
     t_peers = n_x * n_y - 1
     vmem = pl.BlockSpec(memory_space=pltpu.VMEM)
     hbm = pl.BlockSpec(memory_space=pltpu.HBM)
@@ -441,20 +467,20 @@
             pltpu.VMEM((CHUNKS, 2, band, chunk), BF16),
             pltpu.VMEM((CHUNKS, 2, n_x - 1, half, chunk), BF16),
             pltpu.VMEM((col_groups, LANES), F32),
-            pltpu.VMEM((row_groups, LANES), F32),
+            pltpu.VMEM((CHUNKS, groups, LANES), F32),
             pltpu.VMEM((row_groups, LANES), F32),
             pltpu.VMEM((col_groups, LANES), F32),
             pltpu.VMEM((col_groups * 8, LANES), F32),
             pltpu.VMEM((col_groups * 8, LANES), F32),
-            pltpu.VMEM((row_groups, LANES), F32),
-            pltpu.VMEM((ITERS + 1, row_groups, LANES), F32),
-            pltpu.VMEM((ITERS + 1, t_peers, row_groups, LANES), F32),
+            pltpu.VMEM((CHUNKS, groups, LANES), F32),
+            pltpu.VMEM((ITERS + 1, CHUNKS, groups, LANES), F32),
+            pltpu.VMEM((ITERS + 1, CHUNKS, t_peers, groups, LANES), F32),
             pltpu.VMEM((ITERS, col_groups, LANES), F32),
             pltpu.VMEM((ITERS, col_groups, LANES), F32),
             pltpu.VMEM((ITERS, n_z, col_groups, LANES), F32),
             dma((LOADS + 1,)),
-            dma((ITERS + 1,)),
-            dma((ITERS + 1,)),
+            dma((ITERS + 1, CHUNKS)),
+            dma((ITERS + 1, CHUNKS)),
             dma((ITERS,)),
             dma((ITERS,)),
             dma((ITERS,)),

time: 71.2 us -> 70.9 us (level)
  no operation moved by 1% of the time
where the time goes in v6:
time: 70.9 us; the launch traced here: 70.8 us
  Pallas kernels  68.3 us (96%)
  local copies, waits for them, and re-layouts  1.8 us (3%)
    pallas_call x1, Pallas kernels, local(): pl.pallas_call(functools.partial(kernel, cfg), out_shape=shapes, in_specs...  68.3 us
    unnamed x3, local copies, waits for them, and re-layouts  1.8 us

profile of v6, /device:TPU:1, one launch (start us, length us, event | category | flops | bytes accessed | tf_op | source)
XLA Modules:
  0.0 70.8 jit_solution(5815979426674579201)
XLA Ops:
  0.6 68.3 %transport.1 = (bf16[64,512]{1,0:T(8,128)(2,1)S(1)}, f32[4,128]{1,0:T(4,128)S(1)}, f32[8,128]{1,0:T(8,128)S(1)}) custom-call(bf16[512,1024]{1,0:T(8,128)(2,1)} %src_hbm.1, bf16[1024,1024]{1,0:T(8,128)(2,1)} %tgt_hbm.1), custom_call_target="tpu_custom_call" | custom-call | tf_op jit(solution)/shard_map/transport/pallas_call | solution.py:452
  69.0 0.6 copy.8
  69.6 0.6 copy.9
  70.2 0.6 copy.10

commit v7 on v6

--- a/solution.py
+++ b/solution.py
@@ -131,6 +131,17 @@
             barrier, inc=1, device_id=peer, device_id_type=pl.DeviceIdType.MESH
         )
 
+    def score(begin, end, q):
+        dot = lax.dot_general(
+            a[begin:end, :],
+            b[q * share : (q + 1) * share, :],
+            NT_DIMS,
+            preferred_element_type=F32,
+        )
+        scores[begin:end, q * share : (q + 1) * share] = dot * (
+            2.0 * LOG2E / (depth * eps)
+        )
+
     for q in range(LOADS):
         loads[1 + q].wait()
         blocks = range(q * share // LANES, (q + 1) * share // LANES)
@@ -138,13 +149,8 @@
             square_sums(b, c * LANES, tt_ref, c)
         if q == 0:
             loads[0].wait()
-        dot = lax.dot_general(
-            a[...],
-            b[q * share : (q + 1) * share, :],
-            NT_DIMS,
-            preferred_element_type=F32,
-        )
-        scores[:, q * share : (q + 1) * share] = dot * (2.0 * LOG2E / (depth * eps))
+        if q < LOADS - 1:
+            score(0, rows, q)
     h_ref[...] = tt_ref[...] * (-LOG2E / (depth * eps))
 
     groups = chunk // LANES
@@ -224,6 +230,8 @@
         total = tree(jnp.add, [m * jnp.exp2(p - top) for p, m in zip(peaks, masses)])
         out_ref[...] = top + log2(total)
 
+    for n in range(CHUNKS):
+        score(n * chunk, (n + 1) * chunk, LOADS - 1)
     rows_pass(0, 0)
 
     @pl.when(leads)

time: 70.9 us -> 70.2 us (level)
  no operation moved by 1% of the time
where the time goes in v7:
time: 70.2 us; the launch traced here: 70.1 us
  Pallas kernels  67.7 us (96%)
  local copies, waits for them, and re-layouts  1.8 us (3%)
    pallas_call x1, Pallas kernels, local(): pl.pallas_call(functools.partial(kernel, cfg), out_shape=shapes, in_specs...  67.7 us
    unnamed x3, local copies, waits for them, and re-layouts  1.8 us

profile of v7, /device:TPU:1, one launch (start us, length us, event | category | flops | bytes accessed | tf_op | source)
XLA Modules:
  0.0 70.1 jit_solution(9796591500838102993)
XLA Ops:
  0.6 67.7 %transport.1 = (bf16[64,512]{1,0:T(8,128)(2,1)S(1)}, f32[4,128]{1,0:T(4,128)S(1)}, f32[8,128]{1,0:T(8,128)S(1)}) custom-call(bf16[512,1024]{1,0:T(8,128)(2,1)} %src_hbm.1, bf16[1024,1024]{1,0:T(8,128)(2,1)} %tgt_hbm.1), custom_call_target="tpu_custom_call" | custom-call | tf_op jit(solution)/shard_map/transport/pallas_call | solution.py:460
  68.3 0.6 copy.8
  68.9 0.6 copy.9
  69.5 0.6 copy.10
